TPU v7x, 32 devices: a whole 2x2x4 slice. The times are simulated.
32 devices in a mesh: rep: 2 (over y), row: 4 (over z), col: 4 (over x, core).
Axes of the slice: x: 2, y: 2, z: 4, core: 2. Of those that a mesh axis runs over, the one named last changes fastest.
Arguments:
- tokens: bfloat16 [192, 8192], P(('rep', 'row'), 'col'), parts along dimension 0, may hold values from -6 to 6
- w_up: bfloat16 [8192, 16384], P('col', 'row'), may hold values from -0.0625 to 0.0625
- w_down: bfloat16 [16384, 8192], P('row', 'col'), may hold values from -0.046875 to 0.046875
- upstream: bfloat16 [192, 8192], P(('rep', 'row'), 'col'), parts along dimension 0, may hold values from -6 to 6
Outputs:
- layer_out: bfloat16 [192, 8192], P(('rep', 'row'), 'col'), parts along dimension 0
- grad_tokens: bfloat16 [192, 8192], P(('rep', 'row'), 'col'), parts along dimension 0
- grad_up: bfloat16 [16384, 16384], P(('rep', 'col'), 'row'), parts along dimension 0
- grad_down: bfloat16 [32768, 8192], P(('rep', 'row'), 'col'), parts along dimension 0
There are 2 independent parts, one for each index of `rep`. A program takes and returns all parts, laid end to end along the dimension named above; an argument that names none is the same for every part. Nothing has to cross between parts.
All inputs are finite; a program needn't handle non-finite values.
Results may differ from a plain program's by a relative error of at most 0.0051.
Values may be sent and summed in bfloat16 or wider, within the bound.
A program may use at most 192 MiB of HBM per device.

v0:
```python
import jax
import jax.numpy as jnp
from jax import lax
from jax.sharding import PartitionSpec as P

root_half = 0.7071067811865476
inv_root_tau = 0.3989422804014327


def gelu_value(values):
    return 0.5 * values * (1.0 + lax.erf(values * root_half))


def gelu_slope(values):
    return (
        0.5 * (1.0 + lax.erf(values * root_half))
        + values * jnp.exp(-0.5 * values * values) * inv_root_tau
    )


def contract_rows(left, right):
    return lax.dot_general(
        left, right, (((0,), (0,)), ((), ())), preferred_element_type=jnp.float32
    )


def contract_cols(left, right):
    return lax.dot_general(
        left, right, (((1,), (1,)), ((), ())), preferred_element_type=jnp.float32
    )


def shards(tokens, w_up, w_down, upstream):
    gathered, gathered_grad = (
        lax.all_gather(tokens, "row", axis=0, tiled=True),
        lax.all_gather(upstream, "row", axis=0, tiled=True),
    )
    factor = gathered.shape[0] ** (-0.5)
    partial_hidden = jnp.dot(gathered, w_up, preferred_element_type=jnp.float32)
    hidden = lax.psum(partial_hidden, "col")
    activated = gelu_value(hidden).astype(jnp.bfloat16)
    picked = activated
    layer_part = lax.psum_scatter(
        jnp.dot(picked, w_down, preferred_element_type=jnp.float32),
        "row",
        scatter_dimension=0,
        tiled=True,
    )
    partial_slope = contract_cols(gathered_grad, w_down)
    d_act = lax.psum(partial_slope, "col")
    d_hidden = (d_act * gelu_slope(hidden)).astype(jnp.bfloat16)
    grad_down = (contract_rows(activated, gathered_grad) * factor).astype(jnp.bfloat16)
    grad_up = (contract_rows(gathered, d_hidden) * factor).astype(jnp.bfloat16)
    picked = d_hidden
    grad_part = lax.psum_scatter(
        contract_cols(picked, w_up), "row", scatter_dimension=0, tiled=True
    )
    return (layer_part.astype(jnp.bfloat16), grad_part.astype(jnp.bfloat16), grad_up, grad_down)


def solution(mesh):
    placed = (P(("rep", "row"), "col"), P("col", "row"), P("row", "col"), P(("rep", "row"), "col"))
    return jax.shard_map(
        shards,
        mesh=mesh,
        in_specs=placed,
        out_specs=(
            P(("rep", "row"), "col"),
            P(("rep", "row"), "col"),
            P(("rep", "col"), "row"),
            P(("rep", "row"), "col"),
        ),
        check_vma=False,
    )
```

profile of v0, /device:TPU:0, one launch (start us, length us, event | category | flops | bytes accessed | tf_op | source)
XLA Modules:
  0.0 203.2 jit_solution(9005992637484573487)
XLA Ops:
  7.2 0.0 all-reduce.3.cloned.1.call-start
  7.2 16.4 %all_gather.6 = bf16[96,2048]{1,0:T(8,128)(2,1)S(1)} all-gather(bf16[24,2048]{1,0:T(8,128)(2,1)} %param.4), channel_id=1, replica_groups=mesh['rep'=2,'row'=4,'col'=4] {'row'}, dimensions={0}, use_global_device_ids=true | all-gather | bytes 491520 | tf_op jit(solution)/shard_map/all_gather | solution.py:35
  23.7 15.8 %all_gather.7 = bf16[96,2048]{1,0:T(8,128)(2,1)S(1)} all-gather(bf16[24,2048]{1,0:T(8,128)(2,1)} %param.7), channel_id=1, replica_groups=mesh['rep'=2,'row'=4,'col'=4] {'row'}, dimensions={0}, use_global_device_ids=true | all-gather | bytes 491520 | tf_op jit(solution)/shard_map/all_gather | solution.py:36
  39.4 12.2 %fusion.12 = f32[96,4096]{1,0:T(8,128)} fusion(bf16[96,2048]{1,0:T(8,128)(2,1)S(1)} %all_gather.7, bf16[4096,2048]{1,0:T(8,128)(2,1)} %param.6), kind=kOutput, calls=%fused_computation.15 | convolution fusion | flops 1610612736 | bytes 18743296 | tf_op jit(solution)/shard_map/dot_general | solution.py:28
  51.6 9.7 %fusion.11 = f32[96,4096]{1,0:T(8,128)} fusion(bf16[96,2048]{1,0:T(8,128)(2,1)S(1)} %all_gather.6, bf16[2048,4096]{1,0:T(8,128)(2,1)} %param.5), kind=kOutput, calls=%fused_computation.14 | convolution fusion | flops 1610612736 | bytes 18743296 | tf_op jit(solution)/shard_map/dot_general | solution.py:39
  61.3 0.0 all-reduce.3.cloned.1.call-update
  61.3 0.0 reduce-scatter.5.cloned.1.call-start
  61.3 69.7 %all-reduce.3.cloned.1.call-done = (f32[96,4096]{1,0:T(8,128)}, f32[96,4096]{1,0:T(8,128)}) async-done(((f32[96,4096]{1,0:T(8,128)}, f32[96,4096]{1,0:T(8,128)}), (f32[96,4096]{1,0:T(8,128)}, f32[96,4096]{1,0:T(8,128)})) %all-reduce.3.cloned.1.call-update) | async-done | bytes 3145744 | tf_op jit(solution)/shard_map/psum | solution.py:40
  131.0 0.0 copy-start
  131.0 13.0 %fusion.9 = f32[96,2048]{1,0:T(8,128)} fusion(bf16[2048,4096]{1,0:T(8,128)(2,1)} %param.5, f32[96,4096]{1,0:T(8,128)} %get-tuple-element.9, f32[96,4096]{1,0:T(8,128)} %get-tuple-element.8), kind=kOutput, calls=%fused_computation.13 | convolution fusion | flops 1614544896 | bytes 20709376 | tf_op jit(solution)/shard_map/dot_general | solution.py:28
  144.1 0.0 reduce-scatter.5.cloned.1.call-update
  144.1 0.2 reduce-scatter.3.cloned.1.call-start
  144.3 0.0 copy-done
  144.3 9.4 %fusion.7 = f32[96,2048]{1,0:T(8,128)} fusion(bf16[4096,2048]{1,0:T(8,128)(2,1)} %param.6, f32[96,4096]{1,0:T(8,128)S(1)} %copy-done), kind=kOutput, calls=%fused_computation.12 | convolution fusion | flops 1612578816 | bytes 19136512 | tf_op jit(solution)/shard_map/dot_general | solution.py:44
  153.8 0.0 reduce-scatter.3.cloned.1.call-update
  153.8 10.0 %fusion = bf16[2048,4096]{0,1:T(8,128)(2,1)} fusion(bf16[96,2048]{1,0:T(8,128)(2,1)S(1)} %all_gather.6, f32[96,4096]{1,0:T(8,128)} %get-tuple-element.9, f32[96,4096]{1,0:T(8,128)S(1)} %copy-done), kind=kOutput, calls=%fused_computation.2 | convolution fusion | flops 1631322112 | bytes 20316160 | tf_op jit(solution)/shard_map/dot_general | solution.py:22
  163.8 21.2 %copy.8 = bf16[2048,4096]{1,0:T(8,128)(2,1)} copy(bf16[2048,4096]{0,1:T(8,128)(2,1)} %fusion) | data formatting | bytes 33554432
  185.0 8.5 %multiply_convert_fusion = bf16[4096,2048]{1,0:T(8,128)(2,1)} fusion(bf16[96,2048]{1,0:T(8,128)(2,1)S(1)} %all_gather.7, f32[96,4096]{1,0:T(8,128)S(1)} %copy-done), kind=kOutput, calls=%fused_computation | convolution fusion | flops 1629356032 | bytes 18743296 | tf_op jit(solution)/shard_map/dot_general | solution.py:22
  193.6 0.0 reduce-scatter.5.cloned.1.call-done
  193.6 1.6 convert_element_type.24
  195.1 0.0 reduce-scatter.3.cloned.1.call-done
  195.1 1.6 convert_element_type.22
Async XLA Ops:
  7.2 123.8 %all-reduce.3.cloned.1.call-start = ((), (), s32[]{:S(2)}) async-start(), calls=%async_computation.4 | async-start | bytes 6291456 | tf_op jit(solution)/shard_map/psum | solution.py:40
  61.3 132.3 %reduce-scatter.5.cloned.1.call-start = ((), (), s32[]{:S(2)}) async-start(), calls=%async_computation.3 | async-start | bytes 983040 | tf_op jit(solution)/shard_map/reduce_scatter | solution.py:55
  131.0 13.3 %copy-start = (f32[96,4096]{1,0:T(8,128)S(1)}, f32[96,4096]{1,0:T(8,128)}, u32[]{:S(2)}) copy-start(f32[96,4096]{1,0:T(8,128)} %get-tuple-element.8) | copy-start | bytes 4718596
  144.1 51.0 %reduce-scatter.3.cloned.1.call-start = ((), (), s32[]{:S(2)}) async-start(), calls=%async_computation.2 | async-start | bytes 983040 | tf_op jit(solution)/shard_map/reduce_scatter | solution.py:43
Sparse Core Ops, SparseCore 0:
  61.4 69.5 all-reduce.2
  144.2 23.3 reduce-scatter.4
  169.9 22.5 reduce-scatter.2
where the time goes:
time: 204 us; the launch traced here: 203 us
  waiting for transfers between devices  69.7 us (34%)
  matrix products  62.8 us (31%)
  blocking collectives  32.2 us (16%)
  local copies, waits for them, and re-layouts  21.3 us (10%)
  between operations  13.8 us (7%)
  other arithmetic  3.15 us (2%)
    psum x1, waiting for transfers between devices, shards(): hidden = lax.psum(partial_hidden, 'col')  69.7 us
    dot_general x2, matrix products, contract_cols(): lax.dot_general(left, right, (((1,), (1,)), ((), ())), preferred_element_...  25.2 us
    unnamed x3, local copies, waits for them, and re-layouts  21.3 us
    dot_general x2, matrix products, contract_rows(): lax.dot_general(left, right, (((0,), (0,)), ((), ())), preferred_element_...  18.5 us
    all_gather x1, blocking collectives, shards(): lax.all_gather(tokens, 'row', axis=0, tiled=True)  16.4 us
    all_gather x1, blocking collectives, shards(): lax.all_gather(upstream, 'row', axis=0, tiled=True)  15.8 us
    dot_general x1, matrix products, shards(): partial_hidden = jnp.dot(gathered, w_up, preferred_element_type=jnp.float32)  9.68 us
    dot_general x1, matrix products, shards(): jnp.dot(picked, w_down, preferred_element_type=jnp.float32)  9.43 us
  transfers between devices with their start and end apart: 3, of which 1 were waited for; matrix products, arithmetic and copies ran while one was open for 25% of the time, Pallas kernels for 0%

commit v1 on v0

v1 whole, which is shorter than its diff:
```python
import functools

import jax
import jax.numpy as jnp
from jax import lax
from jax.experimental import pallas as pl
from jax.experimental.pallas import tpu as pltpu
from jax.sharding import PartitionSpec as P

MESH = pl.DeviceIdType.MESH
F32, BF16 = jnp.float32, jnp.bfloat16
root_half = 0.7071067811865476
inv_root_tau = 0.3989422804014327


def gelu_value(values):
    return 0.5 * values * (1.0 + lax.erf(values * root_half))


def gelu_slope(values):
    return (
        0.5 * (1.0 + lax.erf(values * root_half))
        + values * jnp.exp(-0.5 * values * values) * inv_root_tau
    )


def contract_rows(left, right):
    return lax.dot_general(left, right, (((0,), (0,)), ((), ())), preferred_element_type=F32)


def contract_cols(left, right):
    return lax.dot_general(left, right, (((1,), (1,)), ((), ())), preferred_element_type=F32)


def remote(src, dst, send, recv, where):
    return pltpu.make_async_remote_copy(
        src_ref=src, dst_ref=dst, send_sem=send, recv_sem=recv,
        device_id=where, device_id_type=MESH,
    )


def exchange_kernel(
    n, chunks, half, tile,
    tok_in, up_in, down_in, cot_in,
    lay_out, gtok_out, tok_out, cot_out, act_out, dh_out,
    wu, wd, tblk, cblk, tok, cot,
    hp, dp, hc, dc, hs, ds_, hx, dx, act, dh,
    lo, gt, lob, gtb, lor, gtr, lfin, gfin,
    wu_sem, wd_sem, own_sem, out_sem,
    t_send, t_recv, c_send, c_recv,
    core_send, core_recv, x_send, x_recv, a_send, a_recv, r_send, r_recv,
):
    row = lax.axis_index("row")
    col = lax.axis_index("col")
    bit = lax.rem(col, 2)
    mate = {"col": col + 1 - 2 * bit}
    across = {"col": lax.rem(col + 2, 4)}
    rows = tok_in.shape[0]
    width = tok_in.shape[1]
    tiles = width // tile

    up_copies = [
        pltpu.make_async_copy(up_in.at[:, pl.ds(g * half, half)], wu.at[g], wu_sem.at[g])
        for g in range(2 * chunks)
    ]
    down_copies = [
        pltpu.make_async_copy(down_in.at[pl.ds(g * half, half), :], wd.at[g], wd_sem.at[g])
        for g in range(2 * chunks)
    ]
    own_t = pltpu.make_async_copy(tok_in, tblk.at[row], own_sem.at[0])
    own_c = pltpu.make_async_copy(cot_in, cblk.at[row], own_sem.at[1])
    own_t.start()
    own_c.start()
    for copy in up_copies:
        copy.start()

    barrier = pltpu.get_barrier_semaphore()
    for step in range(1, n):
        pl.semaphore_signal(
            barrier, inc=1, device_id={"row": lax.rem(row + step, n)}, device_id_type=MESH
        )
    pl.semaphore_signal(barrier, inc=1, device_id=mate, device_id_type=MESH)
    pl.semaphore_signal(barrier, inc=1, device_id=across, device_id_type=MESH)
    pl.semaphore_wait(barrier, n + 1)

    right = {"row": lax.rem(row + 1, n)}
    left = {"row": lax.rem(row + n - 1, n)}

    def send_own(src, blk, send, recv):
        @pl.when(row < n - 1)
        def _():
            remote(src, blk.at[row], send.at[0, row], recv.at[row], right).start()

        @pl.when(row > 0)
        def _():
            remote(src, blk.at[row], send.at[1, row], recv.at[row], left).start()

    def hop(step, blk, send, recv):
        low, high = row - step, row + step

        @pl.when(low >= 0)
        def _():
            remote(blk.at[low], blk.at[low], send.at[0, low], recv.at[low], right).wait_recv()

            @pl.when(row < n - 1)
            def _():
                remote(blk.at[low], blk.at[low], send.at[0, low], recv.at[low], right).start()

        @pl.when(high < n)
        def _():
            remote(blk.at[high], blk.at[high], send.at[1, high], recv.at[high], left).wait_recv()

            @pl.when(row > 0)
            def _():
                remote(blk.at[high], blk.at[high], send.at[1, high], recv.at[high], left).start()

    def close_hops(src, blk, send, recv):
        for b in range(n):
            @pl.when(jnp.logical_and(b <= row, row < n - 1))
            def _():
                remote(blk.at[b], blk.at[b], send.at[0, b], recv.at[b], right).wait_send()

            @pl.when(jnp.logical_and(b >= row, row > 0))
            def _():
                remote(blk.at[b], blk.at[b], send.at[1, b], recv.at[b], left).wait_send()

    def join(blk, whole):
        whole[...] = jnp.concatenate(
            [blk[b].astype(F32) for b in range(n)], axis=0
        ).astype(BF16)

    send_own(tok_in, tblk, t_send, t_recv)
    for step in range(1, n):
        hop(step, tblk, t_send, t_recv)
        if step == n - 2:
            send_own(cot_in, cblk, c_send, c_recv)
    if n < 3:
        send_own(cot_in, cblk, c_send, c_recv)
    for copy in down_copies:
        copy.start()
    own_t.wait()
    join(tblk, tok)
    tok_save = pltpu.make_async_copy(tok, tok_out, out_sem.at[0])
    tok_save.start()

    def to_mate(which, k, part, landing):
        return remote(
            part.at[k, 1 - bit], landing.at[k], core_send.at[which, k], core_recv.at[which, k], mate
        )

    def to_across(which, k, sent, landing):
        return remote(
            sent.at[k], landing.at[k], x_send.at[which, k], x_recv.at[which, k], across
        )

    def to_share(which, k, value):
        return remote(
            value.at[k, bit], value.at[k, bit], a_send.at[which, k], a_recv.at[which, k], mate
        )

    def from_share(which, k, value):
        return remote(
            value.at[k, 1 - bit], value.at[k, 1 - bit],
            a_send.at[which, k], a_recv.at[which, k], mate,
        )

    def pair_sum(which, k, part, landing, sent, arrive):
        to_mate(which, k, part, landing).wait_recv()
        total = part[k, bit] + landing[k]
        part[k, bit] = total
        sent[k] = total.astype(BF16)
        to_across(which, k, sent, arrive).start()

    def finish_hidden(k):
        to_across(0, k, hs, hx).wait_recv()
        hidden = hp[k, bit] + hx[k].astype(F32)
        hp[k, bit] = hidden
        act[k, bit] = gelu_value(hidden).astype(BF16)
        to_share(0, k, act).start()

    def finish_slope(k):
        to_across(1, k, ds_, dx).wait_recv()
        d_act = dp[k, bit] + dx[k].astype(F32)
        dh[k, bit] = (d_act * gelu_slope(hp[k, bit])).astype(BF16)
        to_share(1, k, dh).start()

    for k in range(chunks):
        up_copies[2 * k].wait()
        up_copies[2 * k + 1].wait()
        hp[k, 1 - bit] = jnp.dot(tok[...], wu[2 * k + 1 - bit], preferred_element_type=F32)
        to_mate(0, k, hp, hc).start()
        hp[k, bit] = jnp.dot(tok[...], wu[2 * k + bit], preferred_element_type=F32)
        if 1 <= k + 1 < n and k + 1 <= n - 1:
            hop(k + 1, cblk, c_send, c_recv)
        if k >= 1:
            pair_sum(0, k - 1, hp, hc, hs, hx)
    for step in range(chunks + 1, n):
        hop(step, cblk, c_send, c_recv)
    pair_sum(0, chunks - 1, hp, hc, hs, hx)
    own_c.wait()
    join(cblk, cot)
    cot_save = pltpu.make_async_copy(cot, cot_out, out_sem.at[1])
    cot_save.start()

    for k in range(chunks):
        down_copies[2 * k].wait()
        down_copies[2 * k + 1].wait()
        dp[k, 1 - bit] = contract_cols(cot[...], wd[2 * k + 1 - bit])
        to_mate(1, k, dp, dc).start()
        dp[k, bit] = contract_cols(cot[...], wd[2 * k + bit])
        if k >= 1:
            pair_sum(1, k - 1, dp, dc, ds_, dx)
            finish_hidden(k - 1)
    pair_sum(1, chunks - 1, dp, dc, ds_, dx)
    finish_hidden(chunks - 1)

    def scatter(which, total, out_blk, landing):
        for j in range(tiles):
            for b in range(n):
                out_blk[b, :, pl.ds(j * tile, tile)] = total[j, b * rows:(b + 1) * rows, :].astype(BF16)
        for step in range(1, n):
            to = lax.rem(row + step, n)
            remote(
                out_blk.at[to], landing.at[row],
                r_send.at[which, step], r_recv.at[which, row], {"row": to},
            ).start()

    def collect(which, total, out_blk, landing, final, out, sem):
        for step in range(1, n):
            frm = lax.rem(row + n - step, n)
            remote(
                out_blk.at[frm], landing.at[frm],
                r_send.at[which, step], r_recv.at[which, frm], {"row": frm},
            ).wait_recv()
        for j in range(tiles):
            cols = pl.ds(j * tile, tile)
            value = total[j, pl.ds(pl.multiple_of(row * rows, 8), rows), :]
            for step in range(1, n):
                value = value + landing[lax.rem(row + n - step, n), :, cols].astype(F32)
            final[:, cols] = value.astype(BF16)
        save = pltpu.make_async_copy(final, out, sem)
        save.start()
        return save

    for k in range(chunks):
        from_share(0, k, act).wait_recv()

        @pl.loop(0, tiles)
        def _(j, k=k):
            cols = pl.ds(pl.multiple_of(j * tile, tile), tile)
            term = jnp.dot(act[k, 0], wd[2 * k, :, cols], preferred_element_type=F32)
            term = term + jnp.dot(act[k, 1], wd[2 * k + 1, :, cols], preferred_element_type=F32)
            lo[j] = term if k == 0 else lo[j] + term
    act_save = pltpu.make_async_copy(act, act_out, out_sem.at[2])
    act_save.start()
    scatter(0, lo, lob, lor)

    finish_slope(0)
    for k in range(chunks):
        if k + 1 < chunks:
            finish_slope(k + 1)
        from_share(1, k, dh).wait_recv()

        @pl.loop(0, tiles)
        def _(j, k=k):
            at = pl.ds(pl.multiple_of(j * tile, tile), tile)
            term = contract_cols(dh[k, 0], wu[2 * k, at, :])
            term = term + contract_cols(dh[k, 1], wu[2 * k + 1, at, :])
            gt[j] = term if k == 0 else gt[j] + term
    dh_save = pltpu.make_async_copy(dh, dh_out, out_sem.at[3])
    dh_save.start()
    scatter(1, gt, gtb, gtr)
    lay_save = collect(0, lo, lob, lor, lfin, lay_out, out_sem.at[4])
    gtok_save = collect(1, gt, gtb, gtr, gfin, gtok_out, out_sem.at[5])

    close_hops(tok_in, tblk, t_send, t_recv)
    close_hops(cot_in, cblk, c_send, c_recv)
    for k in range(chunks):
        to_mate(0, k, hp, hc).wait_send()
        to_mate(1, k, dp, dc).wait_send()
        to_across(0, k, hs, hx).wait_send()
        to_across(1, k, ds_, dx).wait_send()
        to_share(0, k, act).wait_send()
        to_share(1, k, dh).wait_send()
    for which, blk in ((0, lob), (1, gtb)):
        for step in range(1, n):
            to = lax.rem(row + step, n)
            remote(
                blk.at[to], blk.at[to],
                r_send.at[which, step], r_recv.at[which, row], {"row": to},
            ).wait_send()
    for save in (tok_save, cot_save, act_save, dh_save, lay_save, gtok_save):
        save.wait()


def grads_kernel(factor, tok, cot, act, dh, up, down, tok_turned):
    @pl.when(pl.program_id(0) == 0)
    def _():
        tok_turned[...] = tok[...].T

    down[...] = (contract_rows(act[0], cot[...]) * factor).astype(BF16)
    up[...] = (jnp.dot(tok_turned[...], dh[0], preferred_element_type=F32) * factor).astype(BF16)


def fused(tokens, w_up, w_down, upstream):
    n = lax.axis_size("row")
    rows, width = tokens.shape
    units = w_up.shape[1]
    count = rows * n
    half = 512
    chunks = units // (2 * half)
    tile = 512
    tiles = width // tile
    dma = pltpu.SemaphoreType.DMA
    anywhere = pl.BlockSpec(memory_space=pl.ANY)
    part = (chunks, 2, count, half)
    own = (chunks, count, half)
    scratch = [
        pltpu.VMEM((2 * chunks, width, half), BF16),
        pltpu.VMEM((2 * chunks, half, width), BF16),
        pltpu.VMEM((n, rows, width), BF16),
        pltpu.VMEM((n, rows, width), BF16),
        pltpu.VMEM((count, width), BF16),
        pltpu.VMEM((count, width), BF16),
        pltpu.VMEM(part, F32),
        pltpu.VMEM(part, F32),
        pltpu.VMEM(own, F32),
        pltpu.VMEM(own, F32),
        pltpu.VMEM(own, BF16),
        pltpu.VMEM(own, BF16),
        pltpu.VMEM(own, BF16),
        pltpu.VMEM(own, BF16),
        pltpu.VMEM(part, BF16),
        pltpu.VMEM(part, BF16),
        pltpu.VMEM((tiles, count, tile), F32),
        pltpu.VMEM((tiles, count, tile), F32),
        pltpu.VMEM((n, rows, width), BF16),
        pltpu.VMEM((n, rows, width), BF16),
        pltpu.VMEM((n, rows, width), BF16),
        pltpu.VMEM((n, rows, width), BF16),
        pltpu.VMEM((rows, width), BF16),
        pltpu.VMEM((rows, width), BF16),
        dma((2 * chunks,)),
        dma((2 * chunks,)),
        dma((2,)),
        dma((6,)),
        dma((2, n)),
        dma((n,)),
        dma((2, n)),
        dma((n,)),
        dma((2, chunks)),
        dma((2, chunks)),
        dma((2, chunks)),
        dma((2, chunks)),
        dma((2, chunks)),
        dma((2, chunks)),
        dma((2, n)),
        dma((2, n)),
    ]
    shape = jax.ShapeDtypeStruct
    layer, grad_tokens, tok, cot, act, dh = pl.pallas_call(
        functools.partial(exchange_kernel, n, chunks, half, tile),
        out_shape=[
            shape((rows, width), BF16),
            shape((rows, width), BF16),
            shape((count, width), BF16),
            shape((count, width), BF16),
            shape(part, BF16),
            shape(part, BF16),
        ],
        in_specs=[anywhere] * 4,
        out_specs=[anywhere] * 6,
        scratch_shapes=scratch,
        compiler_params=pltpu.CompilerParams(
            collective_id=0, has_side_effects=True, vmem_limit_bytes=60 * 1024 * 1024
        ),
        cost_estimate=pl.CostEstimate(
            flops=8 * count * width * units,
            bytes_accessed=4 * width * units,
            transcendentals=0,
        ),
    )(tokens, w_up, w_down, upstream)
    act = act.reshape(2 * chunks, count, half)
    dh = dh.reshape(2 * chunks, count, half)
    step = 256
    per = half // step
    whole = pl.BlockSpec((count, width), lambda g: (0, 0))
    grad_up, grad_down = pl.pallas_call(
        functools.partial(grads_kernel, count ** (-0.5)),
        grid=(units // step,),
        out_shape=[shape((width, units), BF16), shape((units, width), BF16)],
        in_specs=[
            whole,
            whole,
            pl.BlockSpec((1, count, step), lambda g: (g // per, 0, g % per)),
            pl.BlockSpec((1, count, step), lambda g: (g // per, 0, g % per)),
        ],
        out_specs=[
            pl.BlockSpec((width, step), lambda g: (0, g)),
            pl.BlockSpec((step, width), lambda g: (g, 0)),
        ],
        scratch_shapes=[pltpu.VMEM((width, count), BF16)],
        compiler_params=pltpu.CompilerParams(vmem_limit_bytes=32 * 1024 * 1024),
        cost_estimate=pl.CostEstimate(
            flops=4 * count * width * units,
            bytes_accessed=4 * width * units,
            transcendentals=0,
        ),
    )(tok, cot, act, dh)
    return layer, grad_tokens, grad_up, grad_down


def plain(tokens, w_up, w_down, upstream):
    gathered = lax.all_gather(tokens, "row", axis=0, tiled=True)
    gathered_grad = lax.all_gather(upstream, "row", axis=0, tiled=True)
    factor = gathered.shape[0] ** (-0.5)
    hidden = lax.psum(jnp.dot(gathered, w_up, preferred_element_type=F32), "col")
    activated = gelu_value(hidden).astype(BF16)
    layer_part = lax.psum_scatter(
        jnp.dot(activated, w_down, preferred_element_type=F32),
        "row", scatter_dimension=0, tiled=True,
    )
    d_act = lax.psum(contract_cols(gathered_grad, w_down), "col")
    d_hidden = (d_act * gelu_slope(hidden)).astype(BF16)
    grad_down = (contract_rows(activated, gathered_grad) * factor).astype(BF16)
    grad_up = (contract_rows(gathered, d_hidden) * factor).astype(BF16)
    grad_part = lax.psum_scatter(
        contract_cols(d_hidden, w_up), "row", scatter_dimension=0, tiled=True
    )
    return (layer_part.astype(BF16), grad_part.astype(BF16), grad_up, grad_down)


def shards(mesh, tokens, w_up, w_down, upstream):
    width, units = w_up.shape
    count = tokens.shape[0] * mesh.shape["row"]
    fits = (
        mesh.shape["col"] == 4
        and 2 <= mesh.shape["row"] <= 8
        and units % 1024 == 0
        and width % 512 == 0
        and count % 16 == 0
        and tokens.shape[0] % 8 == 0
        and 4 * width * units + 32 * count * units + 24 * count * width <= 56 * 2 ** 20
    )
    return (fused if fits else plain)(tokens, w_up, w_down, upstream)


def solution(mesh):
    placed = (P(("rep", "row"), "col"), P("col", "row"), P("row", "col"), P(("rep", "row"), "col"))
    return jax.shard_map(
        functools.partial(shards, mesh),
        mesh=mesh,
        in_specs=placed,
        out_specs=(
            P(("rep", "row"), "col"),
            P(("rep", "row"), "col"),
            P(("rep", "col"), "row"),
            P(("rep", "row"), "col"),
        ),
        check_vma=False,
    )
```

time: 204 us -> 77.6 us (0.38)
  waiting for transfers between devices: 69.7 us -> 0 us
  Pallas kernels: 0 us -> 68.9 us
  matrix products: 62.8 us -> 0 us
  blocking collectives: 32.2 us -> 0 us
  local copies, waits for them, and re-layouts: 21.3 us -> 7.33 us
  between operations: 13.8 us -> 0.65 us
  other arithmetic: 3.15 us -> 0 us
    psum x1 -> x0, waiting for transfers between devices: 69.7 us -> none  [shards(): hidden = lax.psum(partial_hidden, 'col')]
    pallas_call x0 -> x2, Pallas kernels: none -> 68.9 us  [the longest x1 53.9 us: fused(): pl.pallas_call(functools.partial(exchange_kernel, n, chunks, half, tile),...]
    dot_general x6 -> x0, matrix products: 62.8 us -> none  [the longest x2 25.2 us: contract_cols(): lax.dot_general(left, right, (((1,), (1,)), ((), ())), preferred_element_...]
    all_gather x2 -> x0, blocking collectives: 32.2 us -> none  [the longest x1 16.4 us: shards(): lax.all_gather(tokens, 'row', axis=0, tiled=True)]
    unnamed x3 -> x10, local copies, waits for them, and re-layouts: 21.3 us -> 7.33 us
    convert_element_type x2 -> x0, other arithmetic: 3.15 us -> none  [the longest x1 1.58 us: shards(): grad_part.astype(jnp.bfloat16)]
  transfers between devices with their start and end apart: 3 -> 0, of which waited for: 1 -> 0; matrix products, arithmetic and copies ran while one was open for 25% -> 0% of each run, Pallas kernels for 0% -> 0%
where the time goes in v1:
time: 77.6 us; the launch traced here: 76.9 us
  Pallas kernels  68.9 us (89%)
  local copies, waits for them, and re-layouts  7.33 us (9%)
    pallas_call x1, Pallas kernels, fused(): pl.pallas_call(functools.partial(exchange_kernel, n, chunks, half, tile),...  53.9 us
    pallas_call x1, Pallas kernels, fused(): pl.pallas_call(functools.partial(grads_kernel, count ** (-0.5)), grid=(un...  15.1 us
    unnamed x10, local copies, waits for them, and re-layouts  7.33 us

profile of v1, /device:TPU:0, one launch (start us, length us, event | category | flops | bytes accessed | tf_op | source)
XLA Modules:
  0.0 76.9 jit_solution(8788147772968830527)
XLA Ops:
  0.6 53.9 %shard_map.75 = (bf16[24,2048]{1,0:T(8,128)(2,1)}, bf16[24,2048]{1,0:T(8,128)(2,1)}, bf16[96,2048]{1,0:T(8,128)(2,1)}, bf16[96,2048]{1,0:T(8,128)(2,1)}, bf16[4,...) custom-call(bf16[24,2048]{1,0:T(8,128)(2,1)} %tok_in.1, bf16[2048,4096]{1,0:T(8,128)(2,1)} %up_in.1, ...), custom_call_target="tpu_custom_call" | custom-call | flops 6442450944 | bytes 33554432 | tf_op jit(solution)/shard_map/pallas_call | solution.py:361
  54.5 0.0 copy-start
  54.5 1.1 %copy-done = bf16[4,2,96,512]{3,2,1,0:T(8,128)(2,1)S(1)} copy-done((bf16[4,2,96,512]{3,2,1,0:T(8,128)(2,1)S(1)}, bf16[4,2,96,512]{3,2,1,0:T(8,128)(2,1)}, u32[]{:S(2)}) %copy-start) | copy-done | bytes 786456
  55.6 0.0 copy-start.1
  55.7 1.1 %copy-done.1 = bf16[4,2,96,512]{3,2,1,0:T(8,128)(2,1)S(1)} copy-done((bf16[4,2,96,512]{3,2,1,0:T(8,128)(2,1)S(1)}, bf16[4,2,96,512]{3,2,1,0:T(8,128)(2,1)}, u32[]{:S(2)}) %copy-start.1) | copy-done | bytes 786456
  56.8 0.0 copy-start.2
  56.8 1.0 %copy-done.2 = bf16[96,2048]{1,0:T(8,128)(2,1)S(1)} copy-done((bf16[96,2048]{1,0:T(8,128)(2,1)S(1)}, bf16[96,2048]{1,0:T(8,128)(2,1)}, u32[]{:S(2)}) %copy-start.2) | copy-done | bytes 393240
  57.8 0.0 copy-start.3
  57.8 1.0 %copy-done.3 = bf16[96,2048]{1,0:T(8,128)(2,1)S(1)} copy-done((bf16[96,2048]{1,0:T(8,128)(2,1)S(1)}, bf16[96,2048]{1,0:T(8,128)(2,1)}, u32[]{:S(2)}) %copy-start.3) | copy-done | bytes 393240
  58.8 15.1 %shard_map.76 = (bf16[2048,4096]{1,0:T(8,128)(2,1)}, bf16[4096,2048]{1,0:T(8,128)(2,1)}) custom-call(bf16[96,2048]{1,0:T(8,128)(2,1)S(1)} %copy-done.2, bf16[96,2048]{1,0:T(8,128)(2,1)S(1)} %copy-done.3, bf16[8,96,512]{2,1,0:T(8,128)(2,1)S(1)} %bitcast.2, bf16[8,96,512]{2,1,0:T(8,128)(2,1)S(1)} %bitcast.3), custom_call_target="tpu_custom_call" | custom-call | flops 3221225472 | bytes 33554432 | tf_op jit(solution)/shard_map/pallas_call | solution.py:388
  73.8 1.5 %copy.10 = bf16[24,2048]{1,0:T(8,128)(2,1)} copy(bf16[24,2048]{1,0:T(8,128)(2,1)} %get-tuple-element.24) | data formatting | bytes 196608
  75.4 1.5 %copy.11 = bf16[24,2048]{1,0:T(8,128)(2,1)} copy(bf16[24,2048]{1,0:T(8,128)(2,1)} %get-tuple-element.25) | data formatting | bytes 196608
Async XLA Ops:
  54.5 1.1 %copy-start = (bf16[4,2,96,512]{3,2,1,0:T(8,128)(2,1)S(1)}, bf16[4,2,96,512]{3,2,1,0:T(8,128)(2,1)}, u32[]{:S(2)}) copy-start(bf16[4,2,96,512]{3,2,1,0:T(8,128)(2,1)} %get-tuple-element.16) | copy-start | bytes 2359300
  55.6 1.1 %copy-start.1 = (bf16[4,2,96,512]{3,2,1,0:T(8,128)(2,1)S(1)}, bf16[4,2,96,512]{3,2,1,0:T(8,128)(2,1)}, u32[]{:S(2)}) copy-start(bf16[4,2,96,512]{3,2,1,0:T(8,128)(2,1)} %get-tuple-element.17) | copy-start | bytes 2359300
  56.8 1.0 %copy-start.2 = (bf16[96,2048]{1,0:T(8,128)(2,1)S(1)}, bf16[96,2048]{1,0:T(8,128)(2,1)}, u32[]{:S(2)}) copy-start(bf16[96,2048]{1,0:T(8,128)(2,1)} %get-tuple-element.14.tok) | copy-start | bytes 1179652
  57.8 1.0 %copy-start.3 = (bf16[96,2048]{1,0:T(8,128)(2,1)S(1)}, bf16[96,2048]{1,0:T(8,128)(2,1)}, u32[]{:S(2)}) copy-start(bf16[96,2048]{1,0:T(8,128)(2,1)} %get-tuple-element.15.cot) | copy-start | bytes 1179652

commit v2 on v1

--- a/solution.py
+++ b/solution.py
@@ -42,14 +42,16 @@
 def exchange_kernel(
     n, chunks, half, tile,
     tok_in, up_in, down_in, cot_in,
-    lay_out, gtok_out, tok_out, cot_out, act_out, dh_out,
+    lay_out, tok_out, cot_out, act_out, dh_out, gtb_out, *scratch
+):
+    (
     wu, wd, tblk, cblk, tok, cot,
     hp, dp, hc, dc, hs, ds_, hx, dx, act, dh,
-    lo, gt, lob, gtb, lor, gtr, lfin, gfin,
+    lo, gt, lob, gtb, lor, lfin,
     wu_sem, wd_sem, own_sem, out_sem,
     t_send, t_recv, c_send, c_recv,
     core_send, core_recv, x_send, x_recv, a_send, a_recv, r_send, r_recv,
-):
+    ) = scratch
     row = lax.axis_index("row")
     col = lax.axis_index("col")
     bit = lax.rem(col, 2)
@@ -83,59 +85,28 @@
     pl.semaphore_signal(barrier, inc=1, device_id=across, device_id_type=MESH)
     pl.semaphore_wait(barrier, n + 1)
 
-    right = {"row": lax.rem(row + 1, n)}
-    left = {"row": lax.rem(row + n - 1, n)}
-
-    def send_own(src, blk, send, recv):
-        @pl.when(row < n - 1)
-        def _():
-            remote(src, blk.at[row], send.at[0, row], recv.at[row], right).start()
-
-        @pl.when(row > 0)
-        def _():
-            remote(src, blk.at[row], send.at[1, row], recv.at[row], left).start()
-
-    def hop(step, blk, send, recv):
-        low, high = row - step, row + step
-
-        @pl.when(low >= 0)
-        def _():
-            remote(blk.at[low], blk.at[low], send.at[0, low], recv.at[low], right).wait_recv()
-
-            @pl.when(row < n - 1)
-            def _():
-                remote(blk.at[low], blk.at[low], send.at[0, low], recv.at[low], right).start()
-
-        @pl.when(high < n)
-        def _():
-            remote(blk.at[high], blk.at[high], send.at[1, high], recv.at[high], left).wait_recv()
-
-            @pl.when(row > 0)
-            def _():
-                remote(blk.at[high], blk.at[high], send.at[1, high], recv.at[high], left).start()
-
-    def close_hops(src, blk, send, recv):
-        for b in range(n):
-            @pl.when(jnp.logical_and(b <= row, row < n - 1))
-            def _():
-                remote(blk.at[b], blk.at[b], send.at[0, b], recv.at[b], right).wait_send()
-
-            @pl.when(jnp.logical_and(b >= row, row > 0))
-            def _():
-                remote(blk.at[b], blk.at[b], send.at[1, b], recv.at[b], left).wait_send()
+    def other(step):
+        return lax.rem(row + step, n)
+
+    def greet(step, src, blk, send, recv):
+        to = other(step)
+        return remote(src, blk.at[row], send.at[step], recv.at[row], {"row": to})
+
+    def arrive(step, blk, send, recv):
+        frm = other(step)
+        remote(blk.at[frm], blk.at[frm], send.at[step], recv.at[frm], {"row": frm}).wait_recv()
 
     def join(blk, whole):
         whole[...] = jnp.concatenate(
             [blk[b].astype(F32) for b in range(n)], axis=0
         ).astype(BF16)
 
-    send_own(tok_in, tblk, t_send, t_recv)
-    for step in range(1, n):
-        hop(step, tblk, t_send, t_recv)
-        if step == n - 2:
-            send_own(cot_in, cblk, c_send, c_recv)
-    if n < 3:
-        send_own(cot_in, cblk, c_send, c_recv)
+    for step in range(1, n):
+        greet(step, tok_in, tblk, t_send, t_recv).start()
+    for step in range(1, n):
+        greet(step, cot_in, cblk, c_send, c_recv).start()
+    for step in range(1, n):
+        arrive(step, tblk, t_send, t_recv)
     for copy in down_copies:
         copy.start()
     own_t.wait()
@@ -190,13 +161,11 @@
         hp[k, 1 - bit] = jnp.dot(tok[...], wu[2 * k + 1 - bit], preferred_element_type=F32)
         to_mate(0, k, hp, hc).start()
         hp[k, bit] = jnp.dot(tok[...], wu[2 * k + bit], preferred_element_type=F32)
-        if 1 <= k + 1 < n and k + 1 <= n - 1:
-            hop(k + 1, cblk, c_send, c_recv)
         if k >= 1:
             pair_sum(0, k - 1, hp, hc, hs, hx)
-    for step in range(chunks + 1, n):
-        hop(step, cblk, c_send, c_recv)
     pair_sum(0, chunks - 1, hp, hc, hs, hx)
+    for step in range(1, n):
+        arrive(step, cblk, c_send, c_recv)
     own_c.wait()
     join(cblk, cot)
     cot_save = pltpu.make_async_copy(cot, cot_out, out_sem.at[1])
@@ -269,12 +238,16 @@
             gt[j] = term if k == 0 else gt[j] + term
     dh_save = pltpu.make_async_copy(dh, dh_out, out_sem.at[3])
     dh_save.start()
-    scatter(1, gt, gtb, gtr)
+    for j in range(tiles):
+        for b in range(n):
+            gtb[b, :, pl.ds(j * tile, tile)] = gt[j, b * rows:(b + 1) * rows, :].astype(BF16)
+    gtb_save = pltpu.make_async_copy(gtb, gtb_out, out_sem.at[5])
+    gtb_save.start()
     lay_save = collect(0, lo, lob, lor, lfin, lay_out, out_sem.at[4])
-    gtok_save = collect(1, gt, gtb, gtr, gfin, gtok_out, out_sem.at[5])
-
-    close_hops(tok_in, tblk, t_send, t_recv)
-    close_hops(cot_in, cblk, c_send, c_recv)
+
+    for step in range(1, n):
+        greet(step, tok_in, tblk, t_send, t_recv).wait_send()
+        greet(step, cot_in, cblk, c_send, c_recv).wait_send()
     for k in range(chunks):
         to_mate(0, k, hp, hc).wait_send()
         to_mate(1, k, dp, dc).wait_send()
@@ -282,24 +255,28 @@
         to_across(1, k, ds_, dx).wait_send()
         to_share(0, k, act).wait_send()
         to_share(1, k, dh).wait_send()
-    for which, blk in ((0, lob), (1, gtb)):
+    for which, blk in ((0, lob),):
         for step in range(1, n):
             to = lax.rem(row + step, n)
             remote(
                 blk.at[to], blk.at[to],
                 r_send.at[which, step], r_recv.at[which, row], {"row": to},
             ).wait_send()
-    for save in (tok_save, cot_save, act_save, dh_save, lay_save, gtok_save):
+    for save in (tok_save, cot_save, act_save, dh_save, lay_save, gtb_save):
         save.wait()
 
 
-def grads_kernel(factor, tok, cot, act, dh, up, down, tok_turned):
+def grads_kernel(factor, tok, cot, act, dh, lay, up, down, lay_out):
     @pl.when(pl.program_id(0) == 0)
     def _():
-        tok_turned[...] = tok[...].T
+        lay_out[...] = lay[...]
 
     down[...] = (contract_rows(act[0], cot[...]) * factor).astype(BF16)
-    up[...] = (jnp.dot(tok_turned[...], dh[0], preferred_element_type=F32) * factor).astype(BF16)
+    turned = tok[...].T
+    half = dh.shape[2]
+    for g in range(dh.shape[0]):
+        value = jnp.dot(turned, dh[g], preferred_element_type=F32)
+        up[:, g * half:(g + 1) * half] = (value * factor).astype(BF16)
 
 
 def fused(tokens, w_up, w_down, upstream):
@@ -337,16 +314,14 @@
         pltpu.VMEM((n, rows, width), BF16),
         pltpu.VMEM((n, rows, width), BF16),
         pltpu.VMEM((n, rows, width), BF16),
-        pltpu.VMEM((n, rows, width), BF16),
-        pltpu.VMEM((rows, width), BF16),
         pltpu.VMEM((rows, width), BF16),
         dma((2 * chunks,)),
         dma((2 * chunks,)),
         dma((2,)),
         dma((6,)),
-        dma((2, n)),
         dma((n,)),
-        dma((2, n)),
+        dma((n,)),
+        dma((n,)),
         dma((n,)),
         dma((2, chunks)),
         dma((2, chunks)),
@@ -358,15 +333,15 @@
         dma((2, n)),
     ]
     shape = jax.ShapeDtypeStruct
-    layer, grad_tokens, tok, cot, act, dh = pl.pallas_call(
+    layer, tok, cot, act, dh, partial = pl.pallas_call(
         functools.partial(exchange_kernel, n, chunks, half, tile),
         out_shape=[
-            shape((rows, width), BF16),
             shape((rows, width), BF16),
             shape((count, width), BF16),
             shape((count, width), BF16),
             shape(part, BF16),
             shape(part, BF16),
+            shape((n, rows, width), BF16),
         ],
         in_specs=[anywhere] * 4,
         out_specs=[anywhere] * 6,
@@ -380,33 +355,40 @@
             transcendentals=0,
         ),
     )(tokens, w_up, w_down, upstream)
+    landed = lax.all_to_all(partial, "row", 0, 0, tiled=True)
     act = act.reshape(2 * chunks, count, half)
     dh = dh.reshape(2 * chunks, count, half)
-    step = 256
-    per = half // step
-    whole = pl.BlockSpec((count, width), lambda g: (0, 0))
-    grad_up, grad_down = pl.pallas_call(
+    steps = 2 * chunks
+    wide = width // steps
+    block = pl.BlockSpec((rows, width), lambda g: (0, 0))
+    grad_up, grad_down, layer = pl.pallas_call(
         functools.partial(grads_kernel, count ** (-0.5)),
-        grid=(units // step,),
-        out_shape=[shape((width, units), BF16), shape((units, width), BF16)],
+        grid=(steps,),
+        out_shape=[
+            shape((width, units), BF16),
+            shape((units, width), BF16),
+            shape((rows, width), BF16),
+        ],
         in_specs=[
-            whole,
-            whole,
-            pl.BlockSpec((1, count, step), lambda g: (g // per, 0, g % per)),
-            pl.BlockSpec((1, count, step), lambda g: (g // per, 0, g % per)),
+            pl.BlockSpec((count, wide), lambda g: (0, g)),
+            pl.BlockSpec((count, width), lambda g: (0, 0)),
+            pl.BlockSpec((1, count, half), lambda g: (g, 0, 0)),
+            pl.BlockSpec((steps, count, half), lambda g: (0, 0, 0)),
+            block,
         ],
         out_specs=[
-            pl.BlockSpec((width, step), lambda g: (0, g)),
-            pl.BlockSpec((step, width), lambda g: (g, 0)),
+            pl.BlockSpec((wide, units), lambda g: (g, 0)),
+            pl.BlockSpec((half, width), lambda g: (g, 0)),
+            block,
         ],
-        scratch_shapes=[pltpu.VMEM((width, count), BF16)],
-        compiler_params=pltpu.CompilerParams(vmem_limit_bytes=32 * 1024 * 1024),
+        compiler_params=pltpu.CompilerParams(vmem_limit_bytes=60 * 1024 * 1024),
         cost_estimate=pl.CostEstimate(
             flops=4 * count * width * units,
             bytes_accessed=4 * width * units,
             transcendentals=0,
         ),
-    )(tok, cot, act, dh)
+    )(tok, cot, act, dh, layer)
+    grad_tokens = jnp.sum(landed.astype(F32), axis=0).astype(BF16)
     return layer, grad_tokens, grad_up, grad_down
 
 
@@ -437,6 +419,7 @@
         mesh.shape["col"] == 4
         and 2 <= mesh.shape["row"] <= 8
         and units % 1024 == 0
+        and width % (128 * (units // 512)) == 0
         and width % 512 == 0
         and count % 16 == 0
         and tokens.shape[0] % 8 == 0

time: 77.6 us -> 67 us (0.86)
  Pallas kernels: 68.9 us -> 59.6 us
  local copies, waits for them, and re-layouts: 7.33 us -> 0 us
  starting transfers between devices: 0 us -> 5.72 us
    pallas_call x1, Pallas kernels: 53.9 us -> 46.2 us  [fused(): pl.pallas_call(functools.partial(exchange_kernel, n, chunks, half, tile),...]
    unnamed x10 -> x0, local copies, waits for them, and re-layouts: 7.33 us -> none
    all_to_all x0 -> x1, starting transfers between devices: none -> 5.72 us  [fused(): landed = lax.all_to_all(partial, 'row', 0, 0, tiled=True)]
    pallas_call x1, Pallas kernels: 15.1 us -> 13.5 us  [fused(): pl.pallas_call(functools.partial(grads_kernel, count ** (-0.5)), grid=(st...]
  transfers between devices with their start and end apart: 0 -> 1, of which waited for: 0 -> 0; matrix products, arithmetic and copies ran while one was open for 0% -> 0% of each run, Pallas kernels for 0% -> 20%
where the time goes in v2:
time: 67 us; the launch traced here: 66.7 us
  Pallas kernels  59.6 us (89%)
  starting transfers between devices  5.72 us (9%)
  other arithmetic  0.7 us (1%)
    pallas_call x1, Pallas kernels, fused(): pl.pallas_call(functools.partial(exchange_kernel, n, chunks, half, tile),...  46.2 us
    pallas_call x1, Pallas kernels, fused(): pl.pallas_call(functools.partial(grads_kernel, count ** (-0.5)), grid=(st...  13.5 us
    all_to_all x1, starting transfers between devices, fused(): landed = lax.all_to_all(partial, 'row', 0, 0, tiled=True)  5.72 us
  transfers between devices with their start and end apart: 1, of which 0 were waited for; matrix products, arithmetic and copies ran while one was open for 0% of the time, Pallas kernels for 20%

profile of v2, /device:TPU:0, one launch (start us, length us, event | category | flops | bytes accessed | tf_op | source)
XLA Modules:
  0.0 66.7 jit_solution(14620590013094932224)
XLA Ops:
  0.6 46.2 %shard_map.75 = (bf16[24,2048]{1,0:T(8,128)(2,1)}, bf16[96,2048]{1,0:T(8,128)(2,1)}, bf16[96,2048]{1,0:T(8,128)(2,1)}, bf16[4,2,96,512]{3,2,1,0:T(8,128)(2,1)}, ...) custom-call(bf16[24,2048]{1,0:T(8,128)(2,1)} %tok_in.1, bf16[2048,4096]{1,0:T(8,128)(2,1)} %up_in.1, ...), custom_call_target="tpu_custom_call" | custom-call | flops 6442450944 | bytes 33554432 | tf_op jit(solution)/shard_map/pallas_call | solution.py:336
  46.8 5.7 %all-to-all-start = ((bf16[4,24,2048]{2,1,0:T(8,128)(2,1)}), bf16[4,24,2048]{2,1,0:T(8,128)(2,1)S(1)}, u32[]{:S(2)}, u32[]{:S(2)}) async-start(bf16[4,24,2048]{2,1,0:T(8,128)(2,1)} %get-tuple-element.19), calls=%async_computation | async-start | bytes 786432 | tf_op jit(solution)/shard_map/all_to_all | solution.py:358
  52.5 13.5 %shard_map.76 = (bf16[2048,4096]{1,0:T(8,128)(2,1)}, bf16[4096,2048]{1,0:T(8,128)(2,1)}, bf16[24,2048]{1,0:T(8,128)(2,1)}) custom-call(bf16[96,2048]{1,0:T(8,128)(2,1)} %get-tuple-element.13.tok, bf16[96,2048]{1,0:T(8,128)(2,1)} %get-tuple-element.14.cot, bf16[8,96,512]{2,1,0:T(8,128)(2,1)} %bitcast.2, bf16[8,96,512]{2,1,0:T(8,128)(2,1)} %bitcast.3, ...), custom_call_target="tpu_custom_call" | custom-call | flops 3221225472 | bytes 33554432 | tf_op jit(solution)/shard_map/pallas_call | solution.py:364
  66.0 0.0 all-to-all-done
  66.0 0.7 %reduce_sum.12 = bf16[24,2048]{1,0:T(8,128)(2,1)} reduce(bf16[4,24,2048]{2,1,0:T(8,128)(2,1)S(1)} %all-to-all-done, bf16[]{:T(256)} %constant.2.clone.1), dimensions={0}, to_apply=%region_0.0 | reduce | flops 147456 | bytes 491522 | tf_op jit(solution)/shard_map/reduce_sum | solution.py:391
Async XLA Ops:
  46.8 19.2 %all-to-all-start = ((bf16[4,24,2048]{2,1,0:T(8,128)(2,1)}), bf16[4,24,2048]{2,1,0:T(8,128)(2,1)S(1)}, u32[]{:S(2)}, u32[]{:S(2)}) async-start(bf16[4,24,2048]{2,1,0:T(8,128)(2,1)} %get-tuple-element.19), calls=%async_computation | async-start | bytes 786432 | tf_op jit(solution)/shard_map/all_to_all | solution.py:358
